TPU v7x, 32 devices: a whole 2x2x4 slice. The times are simulated.
32 devices in a mesh: dp: 8 (over y, x, core), axial: 4 (over z).
Axes of the slice: x: 2, y: 2, z: 4, core: 2. Of those that a mesh axis runs over, the one named last changes fastest.
Arguments:
- homolog_activity: bfloat16 [64, 32, 256], P(('dp', 'axial')), parts along dimension 0, may hold values from -6 to 6
- homolog_symbol_ids: int32 [64, 32], P(('dp', 'axial')), parts along dimension 0, may hold values from 0 to 22
- residue_present_mask: int32 [256], P('dp'), parts along dimension 0, may hold values 0 or 1
- pair_state: bfloat16 [256, 32, 128], P(('dp', 'axial')), parts along dimension 0, may hold values from -6 to 6
- pair_valid_mask: int32 [256, 32], P(('dp', 'axial')), parts along dimension 0, may hold values 0 or 1
- symbol_lookup_matrix: bfloat16 [23, 256], replicated, may hold values from -3 to 3
- row_query_weight: bfloat16 [256, 256], replicated, as said below
- horizontal_attention_matrix: bfloat16 [256, 768], replicated, may hold values from -0.375 to 0.375
- pair_bias_weight: bfloat16 [128, 8], replicated, may hold values from -0.5 to 0.5
- horizontal_final_matrix: bfloat16 [256, 256], replicated, may hold values from -0.375 to 0.375
- column_query_weight: bfloat16 [256, 256], replicated, as said below
- vertical_attention_matrix: bfloat16 [256, 768], replicated, may hold values from -0.375 to 0.375
- vertical_final_matrix: bfloat16 [256, 256], replicated, may hold values from -0.375 to 0.375
- tensor_mean_lift_matrix: bfloat16 [256, 64], replicated, may hold values from -0.375 to 0.375
- outer_product_output_weight: bfloat16 [1024, 128], replicated, may hold values from -0.75 to 0.75
- triangle_projection_weight: bfloat16 [128, 256], replicated, may hold values from -0.5 to 0.5
- triangle_projection_gate: bfloat16 [128, 256], replicated, may hold values from -0.5 to 0.5
- triangle_output_gate: bfloat16 [128, 128], replicated, may hold values from -0.5 to 0.5
- triangle_output_weight: bfloat16 [128, 128], replicated, may hold values from -0.5 to 0.5
Outputs:
- alignment_output: bfloat16 [64, 32, 256], P('dp', 'axial'), parts along dimension 0
- pair_output: bfloat16 [256, 32, 128], P(('dp', 'axial')), parts along dimension 0
There are 8 independent parts, one for each index of `dp`. A program takes and returns all parts, laid end to end along the dimension named above; an argument that names none is the same for every part. Nothing has to cross between parts.
Inputs may be any that keep to these rules, and one draw needn't show every extreme that they name: `row_query_weight`: a projection of 256 inputs. `column_query_weight`: a projection of 256 inputs.
All inputs are finite; a program needn't handle non-finite values. No bound on the sum of `pair_valid_mask` on one device may be relied on, other than what follows from the above.
Results may differ from a plain program's by a relative error of at most 0.03.
The roundings to bfloat16 on the way count: a program that leaves them out, or rounds other values in their place, can miss the bound.
Values may be sent and summed in bfloat16 or wider, within the bound.
No kernel may reach another device: no remote copies, remote signals or barrier semaphores. Data moves between devices by JAX's collectives and lax.ppermute only.
A program may use at most 64 MiB of HBM per device.

v0:
```python
import jax
import jax.numpy as jnp
from jax import lax
from jax.sharding import PartitionSpec as P

FOCUS_TOTAL = 8
FOCUS_SIZE = 32
MEAN_HIDDEN_SIZE = 32
C_TRI = 128


def layer_normalize(attended_entries):
    attended_entries = attended_entries.astype(jnp.float32)
    mean = jnp.mean(attended_entries, axis=-1, keepdims=True)
    centred = attended_entries - mean
    var = jnp.mean(centred * centred, axis=-1, keepdims=True)
    return centred * lax.rsqrt(var + 1e-05)


def gated_attend(evoformer_block, extra_axes, w_query, w_kvg, w_out):
    lines_list, residue_length, input_width = evoformer_block.shape
    width = FOCUS_TOTAL * FOCUS_SIZE
    flat = (
        layer_normalize(evoformer_block)
        .astype(jnp.bfloat16)
        .reshape(lines_list * residue_length, input_width)
    )
    query = (
        jnp.dot(flat, w_query, preferred_element_type=jnp.float32) * FOCUS_SIZE ** (-0.5)
    ).astype(jnp.bfloat16)
    query = query.reshape(lines_list, residue_length, FOCUS_TOTAL, FOCUS_SIZE)
    kvg = jnp.dot(flat, w_kvg, preferred_element_type=jnp.float32)
    keys = (
        kvg[:, :width]
        .astype(jnp.bfloat16)
        .reshape(lines_list, residue_length, FOCUS_TOTAL, FOCUS_SIZE)
    )
    attended_entries = (
        kvg[:, width : 2 * width]
        .astype(jnp.bfloat16)
        .reshape(lines_list, residue_length, FOCUS_TOTAL, FOCUS_SIZE)
    )
    gate = jax.nn.sigmoid(kvg[:, 2 * width :]).reshape(
        lines_list, residue_length, FOCUS_TOTAL, FOCUS_SIZE
    )
    scores = (
        jnp.einsum("bihd,bjhd->bhij", query, keys, preferred_element_type=jnp.float32) + extra_axes
    )
    top = jnp.max(scores, axis=-1, keepdims=True)
    expo = jnp.exp(scores - top)
    weights = (expo / jnp.sum(expo, axis=-1, keepdims=True)).astype(jnp.bfloat16)
    mixed = jnp.einsum(
        "bhij,bjhd->bihd", weights, attended_entries, preferred_element_type=jnp.float32
    )
    mixed = (mixed * gate).astype(jnp.bfloat16).reshape(lines_list * residue_length, width)
    return evoformer_block + jnp.dot(mixed, w_out, preferred_element_type=jnp.float32).reshape(
        lines_list, residue_length, input_width
    )


def finish_sums(evoformer_block, triangle_output_weight):
    mixed = layer_normalize(jnp.transpose(evoformer_block, (1, 2, 0))).astype(jnp.bfloat16)
    return jnp.einsum(
        "ijc,cz->ijz", mixed, triangle_output_weight, preferred_element_type=jnp.float32
    )


def local(
    homolog_activity,
    homolog_symbol_ids,
    residue_present_mask,
    pair_state,
    pair_valid_mask,
    symbol_lookup_matrix,
    row_query_weight,
    horizontal_attention_matrix,
    pair_bias_weight,
    horizontal_final_matrix,
    column_query_weight,
    vertical_attention_matrix,
    vertical_final_matrix,
    tensor_mean_lift_matrix,
    outer_product_output_weight,
    triangle_projection_weight,
    triangle_projection_gate,
    triangle_output_gate,
    triangle_output_weight,
):
    sequence_per_device, residue_length, input_width = homolog_activity.shape
    res_dev = pair_state.shape[0]
    group_size = lax.axis_size("axial")
    token_classes = symbol_lookup_matrix.shape[0]
    token_one_hot = (
        homolog_symbol_ids[..., None] == jnp.arange(token_classes, dtype=jnp.int32)
    ).astype(jnp.bfloat16)
    token_embedded = jnp.einsum(
        "slt,tc->slc", token_one_hot, symbol_lookup_matrix, preferred_element_type=jnp.float32
    )
    homolog_starting = homolog_activity.astype(jnp.float32) + token_embedded
    pair_norm = layer_normalize(pair_state).astype(jnp.bfloat16)
    bias_rows = jnp.einsum(
        "ijc,ch->hij", pair_norm, pair_bias_weight, preferred_element_type=jnp.float32
    ).astype(jnp.bfloat16)
    bias_full = lax.all_gather(bias_rows, "axial", axis=1, tiled=True)
    key_bias = 1000000000.0 * (residue_present_mask.astype(jnp.float32) - 1.0)
    extra_axes = bias_full.astype(jnp.float32)[None] + key_bias[None, None, None, :]
    cluster_total = homolog_starting.reshape(
        sequence_per_device // 2, 2, residue_length, input_width
    )
    homolog_across_update = lax.map(
        lambda evoformer_block: gated_attend(
            evoformer_block,
            extra_axes,
            row_query_weight,
            horizontal_attention_matrix,
            horizontal_final_matrix,
        ),
        cluster_total,
    )
    homolog_across_update = homolog_across_update.reshape(
        sequence_per_device, group_size, res_dev, input_width
    ).astype(jnp.bfloat16)
    moved = jnp.swapaxes(
        lax.all_to_all(homolog_across_update, "axial", split_axis=1, concat_axis=0, tiled=True)[
            :, 0
        ],
        0,
        1,
    )
    finished = lax.map(
        lambda item: gated_attend(
            item[None].astype(jnp.float32),
            0.0,
            column_query_weight,
            vertical_attention_matrix,
            vertical_final_matrix,
        )[0],
        moved,
    )
    exchanged = jnp.swapaxes(finished, 0, 1).astype(jnp.bfloat16)[:, None]
    sequence_count = exchanged.shape[0]
    alignment_after_columns = exchanged.reshape(sequence_count, res_dev, input_width)
    tensor_mean_scaler = layer_normalize(alignment_after_columns).astype(jnp.bfloat16)
    split_parts = jnp.einsum(
        "src,cf->rsf",
        tensor_mean_scaler,
        tensor_mean_lift_matrix,
        preferred_element_type=jnp.float32,
    ).astype(jnp.bfloat16)
    first_factor = split_parts[..., :MEAN_HIDDEN_SIZE]
    second_factor = split_parts[..., MEAN_HIDDEN_SIZE:].reshape(
        res_dev, sequence_count * MEAN_HIDDEN_SIZE
    )
    step_rows = 8
    left_blocks = first_factor.reshape(
        res_dev // step_rows, step_rows, sequence_count, MEAN_HIDDEN_SIZE
    )
    piece = lax.all_gather(second_factor, "axial", axis=0, tiled=True)
    count = piece.shape[0]
    right_part = piece.reshape(count, sequence_count, MEAN_HIDDEN_SIZE)

    def one_block(lines_list):
        tensor_mean = (
            jnp.einsum("isc,jsd->ijcd", lines_list, right_part, preferred_element_type=jnp.float32)
            / sequence_count
        )
        tensor_mean = tensor_mean.reshape(
            step_rows, count, MEAN_HIDDEN_SIZE * MEAN_HIDDEN_SIZE
        ).astype(jnp.bfloat16)
        return jnp.einsum(
            "ijf,fz->ijz",
            tensor_mean,
            outer_product_output_weight,
            preferred_element_type=jnp.float32,
        )

    update = lax.map(one_block, left_blocks).reshape(
        res_dev, count, outer_product_output_weight.shape[1]
    )
    pair_one = pair_state.astype(jnp.float32) + update
    tri_norm = layer_normalize(pair_one).astype(jnp.bfloat16)
    proj = jnp.einsum(
        "ikc,cf->fik", tri_norm, triangle_projection_weight, preferred_element_type=jnp.float32
    )
    gates = jnp.einsum(
        "ikc,cf->fik", tri_norm, triangle_projection_gate, preferred_element_type=jnp.float32
    )
    both = (jax.nn.sigmoid(gates) * proj * pair_valid_mask.astype(jnp.float32)[None]).astype(
        jnp.bfloat16
    )
    left_tri = both[:C_TRI]
    right_tri = both[C_TRI:]
    moved_left, moved_right = (
        lax.all_to_all(left_tri, "axial", split_axis=0, concat_axis=1, tiled=True),
        lax.all_to_all(right_tri, "axial", split_axis=0, concat_axis=1, tiled=True),
    )
    partial_sum = jnp.einsum(
        "cik,cjk->cij", moved_left, moved_right, preferred_element_type=jnp.float32
    )
    tri_sum = lax.all_to_all(
        partial_sum.astype(jnp.bfloat16), "axial", split_axis=1, concat_axis=0, tiled=True
    ).astype(partial_sum.dtype)
    tri_update = finish_sums(tri_sum, triangle_output_weight)
    out_gate = jax.nn.sigmoid(
        jnp.einsum(
            "ijc,cz->ijz", tri_norm, triangle_output_gate, preferred_element_type=jnp.float32
        )
    )
    pair_output = (pair_one + out_gate * tri_update).astype(jnp.bfloat16)
    return (alignment_after_columns, pair_output)


def solution(mesh):
    return jax.shard_map(
        local,
        mesh=mesh,
        in_specs=(
            P(("dp", "axial"), None, None),
            P(("dp", "axial"), None),
            P("dp"),
            P(("dp", "axial"), None, None),
            P(("dp", "axial"), None),
            P(),
            P(),
            P(),
            P(),
            P(),
            P(),
            P(),
            P(),
            P(),
            P(),
            P(),
            P(),
            P(),
            P(),
        ),
        out_specs=(P("dp", "axial", None), P(("dp", "axial"), None, None)),
        check_vma=False,
    )
```

profile of v0, /device:TPU:0, one launch (start us, length us, event | category | flops | bytes accessed | tf_op | source)
XLA Modules:
  0.0 103.0 jit_solution(2722796312247533505)
XLA Ops:
  0.6 1.1 %fusion.110 = (f32[2,32]{1,0:T(2,128)S(1)}, f32[2,32,256]{2,1,0:T(8,128)S(1)}) fusion(bf16[23,256]{1,0:T(8,128)(2,1)} %param.26, s32[2,32]{1,0:T(2,128)} %param.22, bf16[2,32,256]{2,1,0:T(8,128)(2,1)} %param.21), kind=kOutput, calls=%fused_computation.142 | convolution fusion | flops 804224 | bytes 110592 | tf_op jit(solution)/shard_map/slt,tc->slc/dot_general | solution.py:96
  2.4 1.0 %fusion.53 = bf16[64,256]{1,0:T(8,128)(2,1)S(1)} fusion(bf16[64,256]{1,0:T(8,128)(2,1)S(1)} %bitcast.154, bf16[256,256]{1,0:T(8,128)(2,1)} %param.27), kind=kOutput, calls=%fused_computation.59 | convolution fusion | flops 8421376 | bytes 196608 | tf_op jit(solution)/shard_map/while/body/eval_jaxpr/dot_general | solution.py:29
  3.6 0.9 convert_reduce_fusion.1
  4.6 1.0 fusion.65
  5.6 1.1 %fusion.56 = bf16[8,8,32]{2,0,1:T(8,128)(2,1)S(1)} fusion(bf16[8,32,128]{2,1,0:T(8,128)(2,1)} %param.24, f32[8,32]{1,0:T(8,128)S(1)} %add_rsqrt_fusion.4, f32[8,32]{1,0:T(8,128)S(1)} %broadcast_multiply_fusion.4, bf16[128,8]{0,1:T(8,128)(2,1)} %param.29), kind=kOutput, calls=%fused_computation.64 | convolution fusion | flops 657408 | bytes 73728 | tf_op jit(solution)/shard_map/ijc,ch->hij/dot_general | solution.py:101
  6.7 14.9 %all_gather.6 = bf16[8,32,32]{2,0,1:T(8,128)(2,1)S(1)} all-gather(bf16[8,8,32]{2,0,1:T(8,128)(2,1)S(1)} %fusion.56), channel_id=1, replica_groups=mesh['dp'=8,'axial'=4] {'axial'}, dimensions={1}, use_global_device_ids=true | all-gather | bytes 20480 | tf_op jit(solution)/shard_map/all_gather | solution.py:104
  21.7 0.7 add_multiply_fusion
  23.6 0.6 copy.73
  24.3 4.7 %all-to-all-start = ((bf16[2,4,8,256]{3,2,0,1:T(8,128)(2,1)}), bf16[2,4,8,256]{3,2,0,1:T(8,128)(2,1)S(1)}, u32[]{:S(2)}, u32[]{:S(2)}) async-start(bf16[2,4,8,256]{3,2,0,1:T(8,128)(2,1)} %copy.73), calls=%async_computation | async-start | bytes 65536 | tf_op jit(solution)/shard_map/all_to_all | solution.py:124
  29.0 5.6 %all-to-all-done = bf16[2,4,8,256]{3,2,0,1:T(8,128)(2,1)S(1)} async-done(((bf16[2,4,8,256]{3,2,0,1:T(8,128)(2,1)}), bf16[2,4,8,256]{3,2,0,1:T(8,128)(2,1)S(1)}, u32[]{:S(2)}, u32[]{:S(2)}) %all-to-all-start) | async-done | bytes 32800 | tf_op jit(solution)/shard_map/all_to_all | solution.py:124
  34.7 15.4 %while.2 = (s32[]{:T(128)}, bf16[8,8,256]{2,0,1:T(8,128)(2,1)S(1)}, bf16[8,8,256]{2,1,0:T(8,128)(2,1)S(1)}, bf16[256,768]{1,0:T(8,128)(2,1)S(1)}, bf16[256,256]{...) while((s32[]{:T(128)}, bf16[8,8,256]{2,0,1:T(8,128)(2,1)S(1)}, ...), condition=%wide.region_11.12_spmd, body=%wide.region_6.11_spmd.sunk | while | flops 5399128 | bytes 867149 | solution.py:130
  50.8 13.1 %all_gather.7 = bf16[32,256]{1,0:T(8,128)(2,1)S(1)} all-gather(bf16[8,256]{1,0:T(8,128)(2,1)S(1)} %reshape.196), channel_id=1, replica_groups=mesh['dp'=8,'axial'=4] {'axial'}, dimensions={0}, use_global_device_ids=true | all-gather | bytes 20480 | tf_op jit(solution)/shard_map/all_gather | solution.py:158
  64.0 2.1 %fusion.36 = bf16[8,32,32,32]{2,3,0,1:T(8,128)(2,1)} fusion(bf16[32,8,32,1]{2,1,0,3:T(8,128)(2,1)S(1)} %reshape.204, bf16[8,8,32]{2,0,1:T(8,128)(2,1)S(1)} %get-tuple-element.91), kind=kOutput, calls=%fused_computation.32 | convolution fusion | flops 4718592 | bytes 544768 | tf_op jit(solution)/shard_map/while/body/eval_jaxpr/isc,jsd->ijcd/dot_general | solution.py:164
  66.2 3.0 %copy.78 = bf16[8,32,32,32]{3,2,1,0:T(8,128)(2,1)S(1)} copy(bf16[8,32,32,32]{2,3,0,1:T(8,128)(2,1)} %fusion.36) | data formatting | bytes 1048576 | tf_op jit(solution)/shard_map/while/body/eval_jaxpr/convert_element_type | solution.py:169
  69.3 2.2 %convert_element_type.144 = bf16[8,32,1024]{2,1,0:T(8,128)(2,1)S(1)} reshape(bf16[8,32,32,32]{3,2,1,0:T(8,128)(2,1)S(1)} %copy.78) | data formatting | bytes 1048576 | tf_op jit(solution)/shard_map/while/body/eval_jaxpr/convert_element_type | solution.py:169
  71.5 0.4 fusion.113
  72.9 0.9 reshape.214
  73.8 3.3 %all-to-all-start.1 = ((bf16[4,2,4096]{2,1,0:T(2,128)(2,1)}), bf16[4,2,4096]{2,1,0:T(2,128)(2,1)S(1)}, u32[]{:S(2)}, u32[]{:S(2)}) async-start(bf16[4,2,4096]{2,1,0:T(2,128)(2,1)} %reshape.214), calls=%async_computation.1 | async-start | bytes 131072 | tf_op jit(solution)/shard_map/all_to_all | solution.py:194
  77.3 0.9 reshape.212
  78.2 4.6 %all-to-all-done.1 = bf16[4,2,4096]{2,1,0:T(2,128)(2,1)S(1)} async-done(((bf16[4,2,4096]{2,1,0:T(2,128)(2,1)}), bf16[4,2,4096]{2,1,0:T(2,128)(2,1)S(1)}, u32[]{:S(2)}, u32[]{:S(2)}) %all-to-all-start.1) | async-done | bytes 65568 | tf_op jit(solution)/shard_map/all_to_all | solution.py:194
  82.8 3.3 %all-to-all-start.2 = ((bf16[4,2,4096]{2,1,0:T(2,128)(2,1)}), bf16[4,2,4096]{2,1,0:T(2,128)(2,1)S(1)}, u32[]{:S(2)}, u32[]{:S(2)}) async-start(bf16[4,2,4096]{2,1,0:T(2,128)(2,1)} %reshape.212), calls=%async_computation.2 | async-start | bytes 131072 | tf_op jit(solution)/shard_map/all_to_all | solution.py:195
  86.3 5.5 %all-to-all-done.2 = bf16[4,2,4096]{2,1,0:T(2,128)(2,1)S(1)} async-done(((bf16[4,2,4096]{2,1,0:T(2,128)(2,1)}), bf16[4,2,4096]{2,1,0:T(2,128)(2,1)S(1)}, u32[]{:S(2)}, u32[]{:S(2)}) %all-to-all-start.2) | async-done | bytes 65568 | tf_op jit(solution)/shard_map/all_to_all | solution.py:195
  92.7 8.1 %all_to_all.60 = bf16[4,2,4096]{2,1,0:T(2,128)(2,1)S(1)} all-to-all(bf16[4,2,4096]{2,1,0:T(2,128)(2,1)S(1)} %reshape.216), channel_id=1, replica_groups=mesh['dp'=8,'axial'=4] {'axial'}, dimensions={0} | all-to-all | bytes 131072 | tf_op jit(solution)/shard_map/all_to_all | solution.py:200
  102.1 0.9 fusion.52
  (234 shorter events, 21.2 us)
Async XLA Ops:
  0.6 1.4 %copy-start = (bf16[256,768]{1,0:T(8,128)(2,1)S(1)}, bf16[256,768]{1,0:T(8,128)(2,1)}, u32[]{:S(2)}) copy-start(bf16[256,768]{1,0:T(8,128)(2,1)} %param.28) | copy-start | bytes 1179652
  5.6 17.8 %copy-start.6 = (bf16[256,256]{1,0:T(8,128)(2,1)S(1)}, bf16[256,256]{1,0:T(8,128)(2,1)}, u32[]{:S(2)}) copy-start(bf16[256,256]{1,0:T(8,128)(2,1)} %param.30) | copy-start | bytes 393220
  22.3 6.7 %copy-start.9 = (s32[8,32]{1,0:T(8,128)S(1)}, s32[8,32]{1,0:T(8,128)}, u32[]{:S(2)}) copy-start(s32[8,32]{1,0:T(8,128)} %param.25) | copy-start | bytes 3076
  22.4 12.2 %copy-start.1 = (bf16[256,768]{1,0:T(8,128)(2,1)S(1)}, bf16[256,768]{1,0:T(8,128)(2,1)}, u32[]{:S(2)}) copy-start(bf16[256,768]{1,0:T(8,128)(2,1)} %param.32) | copy-start | bytes 1179652
  22.5 12.2 %copy-start.2 = (bf16[256,256]{1,0:T(8,128)(2,1)S(1)}, bf16[256,256]{1,0:T(8,128)(2,1)}, u32[]{:S(2)}) copy-start(bf16[256,256]{1,0:T(8,128)(2,1)} %param.33) | copy-start | bytes 393220
  22.5 12.2 %copy-start.10 = (bf16[256,256]{1,0:T(8,128)(2,1)S(1)}, bf16[256,256]{1,0:T(8,128)(2,1)}, u32[]{:S(2)}) copy-start(bf16[256,256]{1,0:T(8,128)(2,1)} %param.31) | copy-start | bytes 393220
  24.3 10.4 %all-to-all-start = ((bf16[2,4,8,256]{3,2,0,1:T(8,128)(2,1)}), bf16[2,4,8,256]{3,2,0,1:T(8,128)(2,1)S(1)}, u32[]{:S(2)}, u32[]{:S(2)}) async-start(bf16[2,4,8,256]{3,2,0,1:T(8,128)(2,1)} %copy.73), calls=%async_computation | async-start | bytes 65536 | tf_op jit(solution)/shard_map/all_to_all | solution.py:124
  34.7 15.7 %copy-start.12 = (bf16[256,64]{0,1:T(8,128)(2,1)S(1)}, bf16[256,64]{0,1:T(8,128)(2,1)}, u32[]{:S(2)}) copy-start(bf16[256,64]{0,1:T(8,128)(2,1)} %param.34) | copy-start | bytes 98308
  50.1 19.1 %copy-start.5 = (bf16[8,8,256]{2,0,1:T(8,128)(2,1)}, bf16[8,8,256]{2,0,1:T(8,128)(2,1)S(1)}, u32[]{:S(2)}) copy-start(bf16[8,8,256]{2,0,1:T(8,128)(2,1)S(1)} %get-tuple-element.65) | copy-start | bytes 98308
  69.2 2.3 %copy-start.3 = (bf16[8,32,128]{2,1,0:T(8,128)(2,1)S(1)}, bf16[8,32,128]{2,1,0:T(8,128)(2,1)}, u32[]{:S(2)}) copy-start(bf16[8,32,128]{2,1,0:T(8,128)(2,1)} %param.24) | copy-start | bytes 196612
  69.2 2.3 %copy-start.4 = (bf16[1024,128]{1,0:T(8,128)(2,1)S(1)}, bf16[1024,128]{1,0:T(8,128)(2,1)}, u32[]{:S(2)}) copy-start(bf16[1024,128]{1,0:T(8,128)(2,1)} %param.35) | copy-start | bytes 786436
  69.2 2.9 %copy-start.11 = (bf16[128,256]{1,0:T(8,128)(2,1)S(1)}, bf16[128,256]{1,0:T(8,128)(2,1)}, u32[]{:S(2)}) copy-start(bf16[128,256]{1,0:T(8,128)(2,1)} %param.37) | copy-start | bytes 196612
  69.3 3.1 %copy-start.7 = (bf16[128,256]{1,0:T(8,128)(2,1)S(1)}, bf16[128,256]{1,0:T(8,128)(2,1)}, u32[]{:S(2)}) copy-start(bf16[128,256]{1,0:T(8,128)(2,1)} %param.36) | copy-start | bytes 196612
  73.8 9.0 %all-to-all-start.1 = ((bf16[4,2,4096]{2,1,0:T(2,128)(2,1)}), bf16[4,2,4096]{2,1,0:T(2,128)(2,1)S(1)}, u32[]{:S(2)}, u32[]{:S(2)}) async-start(bf16[4,2,4096]{2,1,0:T(2,128)(2,1)} %reshape.214), calls=%async_computation.1 | async-start | bytes 131072 | tf_op jit(solution)/shard_map/all_to_all | solution.py:194
  82.8 9.0 %all-to-all-start.2 = ((bf16[4,2,4096]{2,1,0:T(2,128)(2,1)}), bf16[4,2,4096]{2,1,0:T(2,128)(2,1)S(1)}, u32[]{:S(2)}, u32[]{:S(2)}) async-start(bf16[4,2,4096]{2,1,0:T(2,128)(2,1)} %reshape.212), calls=%async_computation.2 | async-start | bytes 131072 | tf_op jit(solution)/shard_map/all_to_all | solution.py:195
  92.3 9.6 %copy-start.8 = (bf16[128,128]{1,0:T(8,128)(2,1)S(1)}, bf16[128,128]{1,0:T(8,128)(2,1)}, u32[]{:S(2)}) copy-start(bf16[128,128]{1,0:T(8,128)(2,1)} %param.39) | copy-start | bytes 98308
  92.3 9.9 %copy-start.13 = (bf16[128,128]{1,0:T(8,128)(2,1)S(1)}, bf16[128,128]{1,0:T(8,128)(2,1)}, u32[]{:S(2)}) copy-start(bf16[128,128]{1,0:T(8,128)(2,1)} %param.38) | copy-start | bytes 98308
where the time goes:
time: 104 us; the launch traced here: 103 us
  blocking collectives  36.1 us (35%)
  matrix products  17 us (16%)
  waiting for transfers between devices  15.8 us (15%)
  local copies, waits for them, and re-layouts  14.8 us (14%)
  starting transfers between devices  11.3 us (11%)
  other arithmetic  6.46 us (6%)
  between operations  1.18 us (1%)
    all_gather x1, blocking collectives, local(): bias_full = lax.all_gather(bias_rows, 'axial', axis=1, tiled=True)  14.9 us
    all_gather x1, blocking collectives, local(): piece = lax.all_gather(second_factor, 'axial', axis=0, tiled=True)  13.1 us
    all_to_all x1, blocking collectives, local(): lax.all_to_all(partial_sum.astype(jnp.bfloat16), 'axial', split_axis=1, c...  8.11 us
    all_to_all x1, waiting for transfers between devices, local(): lax.all_to_all(homolog_across_update, 'axial', split_axis=1, concat_axis=...  5.65 us
    all_to_all x1, waiting for transfers between devices, local(): lax.all_to_all(right_tri, 'axial', split_axis=0, concat_axis=1, tiled=True)  5.52 us
    convert_element_type x2, local copies, waits for them, and re-layouts, one_block(): tensor_mean = tensor_mean.reshape(step_rows, count, MEAN_HIDDEN_SIZE * ME...  5.28 us
    all_to_all x1, starting transfers between devices, local(): lax.all_to_all(homolog_across_update, 'axial', split_axis=1, concat_axis=...  4.74 us
    all_to_all x1, waiting for transfers between devices, local(): lax.all_to_all(left_tri, 'axial', split_axis=0, concat_axis=1, tiled=True)  4.59 us
  transfers between devices with their start and end apart: 3, of which 3 were waited for; matrix products, arithmetic and copies ran while one was open for 1% of the time, Pallas kernels for 0%

commit v1 on v0

--- a/solution.py
+++ b/solution.py
@@ -1,6 +1,10 @@
+import functools
+
 import jax
 import jax.numpy as jnp
 from jax import lax
+from jax.experimental import pallas as pl
+from jax.experimental.pallas import tpu as pltpu
 from jax.sharding import PartitionSpec as P
 
 FOCUS_TOTAL = 8
@@ -65,7 +69,7 @@
     )
 
 
-def local(
+def local_sharded(
     homolog_activity,
     homolog_symbol_ids,
     residue_present_mask,
@@ -210,31 +214,358 @@
     return (alignment_after_columns, pair_output)
 
 
+BF16 = jnp.bfloat16
+F32 = jnp.float32
+VMEM_LIMIT = 40 * 1024 * 1024
+
+
+def mul(lhs, rhs, over=((1,), (0,))):
+    return lax.dot_general(lhs, rhs, (over, ((), ())), preferred_element_type=F32)
+
+
+def iota(shape, axis):
+    return lax.broadcasted_iota(jnp.int32, shape, axis)
+
+
+def zero_one(condition):
+    return jnp.where(condition, 1.0, 0.0).astype(BF16)
+
+
+def normal(x):
+    mean = jnp.mean(x, axis=-1, keepdims=True)
+    centred = x - mean
+    var = jnp.mean(centred * centred, axis=-1, keepdims=True)
+    return centred * lax.rsqrt(var + 1e-05)
+
+
+def sigmoid(x):
+    return 1.0 / (1.0 + jnp.exp(-x))
+
+
+def column_softmax(scores):
+    expo = jnp.exp(scores - jnp.max(scores, axis=0, keepdims=True))
+    return expo * (1.0 / jnp.sum(expo, axis=0, keepdims=True))
+
+
+def head_masks(width):
+    return [
+        zero_one(iota((1, width), 1) // FOCUS_SIZE == h) for h in range(FOCUS_TOTAL)
+    ]
+
+
+def packet_rows(residues, res_dev):
+    return residues + 16 if res_dev <= 8 else residues + 2 * res_dev
+
+
+def packet_kernel(pair_ref, ids_ref, valid_ref, weight_ref, packet_ref, held):
+    rows, residues, width = pair_ref.shape
+    lanes = FOCUS_TOTAL * rows
+    flat = normal(pair_ref[...].astype(F32).reshape(rows * residues, width)).astype(BF16)
+    spread = zero_one(iota((FOCUS_TOTAL, lanes), 1) // rows == iota((FOCUS_TOTAL, lanes), 0))
+    weight = mul(weight_ref[...], spread)
+    row_of = iota((width, lanes), 1) % rows
+    bias = jnp.zeros((residues, lanes), F32)
+    for i in range(rows):
+        one_row = jnp.where(row_of == i, weight, 0.0).astype(BF16)
+        bias += mul(flat[i * residues : (i + 1) * residues], one_row)
+    held[...] = jnp.zeros_like(held)
+    held[0:residues, 0:lanes] = bias
+    held[residues : residues + rows, 0:residues] = valid_ref[...].astype(F32)
+    held[residues + 8 : residues + 8 + ids_ref.shape[0], 0:residues] = ids_ref[...].astype(F32)
+    packet_ref[...] = held[...].astype(BF16)
+
+
+def project(x, w_query, w_kvg):
+    width = FOCUS_TOTAL * FOCUS_SIZE
+    flat = normal(x).astype(BF16)
+    query = (mul(flat, w_query[...]) * FOCUS_SIZE ** (-0.5)).astype(BF16)
+    keys = mul(flat, w_kvg[:, :width]).astype(BF16)
+    values = mul(flat, w_kvg[:, width : 2 * width]).astype(BF16)
+    gate = sigmoid(mul(flat, w_kvg[:, 2 * width :]))
+    return query, keys, values, gate
+
+
+def msa_kernel(n, *refs):
+    acts, packets, refs = refs[:n], refs[n : 2 * n], refs[2 * n :]
+    (present, table, row_q, row_kvg, row_out, col_q, col_kvg, col_out, lift, outer_w), refs = (
+        refs[:10],
+        refs[10:],
+    )
+    align_ref, update_ref, start, lifted = refs
+    per, residues, width = acts[0].shape
+    count = per * n
+    res_dev = residues // n
+    tokens = count * residues
+    lanes = FOCUS_TOTAL * residues
+    me = lax.axis_index("axial")
+    masks = head_masks(width)
+    kinds = table.shape[0]
+
+    place = iota((FOCUS_TOTAL * res_dev, lanes), 0)
+    place = (place // res_dev) * residues + place % res_dev - iota(place.shape, 1)
+    extra = jnp.zeros((residues, lanes), F32)
+    for r in range(n):
+        owner = lax.rem(me + r, n)
+        packet = packets[r][...].astype(F32)
+        bias = packet[:residues, : FOCUS_TOTAL * res_dev].astype(BF16)
+        extra += mul(bias, zero_one(place == -owner * res_dev))
+        for q in range(per):
+            ids = packet[residues + 8 + q : residues + 9 + q, :residues]
+            hot = zero_one(iota((kinds, residues), 0).astype(F32) == ids)
+            start[pl.ds(pl.multiple_of((owner * per + q) * residues, residues), residues), :] = (
+                acts[r][q].astype(F32) + mul(hot, table[...], ((0,), (0,)))
+            )
+    shown = mul(present[...].astype(F32).astype(BF16), jnp.ones((1, lanes), BF16), ((0,), (0,)))
+    extra = extra + 1000000000.0 * (shown - 1.0)
+
+    zero = start[...]
+    query, keys, values, gate = project(zero, row_q, row_kvg)
+    rows = []
+    for s in range(count):
+        here = slice(s * residues, (s + 1) * residues)
+        spread = jnp.concatenate([query[here] * mask for mask in masks], axis=0)
+        weights = column_softmax(mul(keys[here], spread, ((1,), (1,))) + extra).astype(BF16)
+        heads = mul(weights, values[here], ((0,), (0,)))
+        mixed = jnp.zeros((residues, width), F32)
+        for h in range(FOCUS_TOTAL):
+            part = heads[h * residues : (h + 1) * residues]
+            mixed = jnp.where(iota((1, width), 1) // FOCUS_SIZE == h, part, mixed)
+        rows.append(mixed)
+    mixed = (jnp.concatenate(rows, axis=0) * gate).astype(BF16)
+    msa_one = (zero + mul(mixed, row_out[...])).astype(BF16)
+
+    row_at, lane_at = iota((tokens, tokens), 0), iota((tokens, tokens), 1)
+    turn = zero_one(lane_at == (row_at % count) * residues + row_at // count)
+    one = mul(turn, msa_one)
+    query, keys, values, gate = project(one, col_q, col_kvg)
+    group = min(tokens, 128)
+    sites = group // count
+    same = iota((sites, count, group), 2) // count == iota((sites, count, group), 0)
+    groups = []
+    for g in range(tokens // group):
+        here = slice(g * group, (g + 1) * group)
+        all_weights, all_values = [], []
+        for mask in masks:
+            scores = mul(keys[here], query[here] * mask, ((1,), (1,)))
+            scores = jnp.sum(jnp.where(same, scores.reshape(sites, count, group), 0.0), axis=0)
+            weights = column_softmax(scores)
+            weights = jnp.where(same, weights[None], 0.0).reshape(group, group)
+            all_weights.append(weights.astype(BF16))
+            all_values.append(values[here] * mask)
+        groups.append(
+            mul(
+                jnp.concatenate(all_weights, axis=0),
+                jnp.concatenate(all_values, axis=0),
+                ((0,), (0,)),
+            )
+        )
+    mixed = (jnp.concatenate(groups, axis=0) * gate).astype(BF16)
+    align = (one + mul(mixed, col_out[...])).astype(BF16)
+    own = count * res_dev
+    row_at, lane_at = iota((own, tokens), 0), iota((own, tokens), 1)
+    pick = zero_one(
+        lane_at == (row_at % res_dev + me * res_dev) * count + row_at // res_dev
+    )
+    align_ref[...] = mul(pick, align).reshape(count, res_dev, width).astype(BF16)
+
+    opm = mul(normal(align.astype(F32)).astype(BF16), lift[...]).astype(BF16)
+    hidden = MEAN_HIDDEN_SIZE
+    deep = hidden * count
+    spread = zero_one(
+        iota((2 * hidden, deep), 1) // count == iota((2 * hidden, deep), 0)
+    )
+    left = mul(opm, spread)
+    left = jnp.where(
+        iota((tokens, deep), 0) % count == iota((tokens, deep), 1) % count, left, 0.0
+    ).astype(BF16)
+    gather = zero_one(iota((residues, tokens), 1) // count == iota((residues, tokens), 0))
+    left = mul(gather, left).astype(BF16)
+    right = opm[:, hidden:]
+    for c in range(hidden):
+        lifted[c] = mul(right, outer_w[c * hidden : (c + 1) * hidden, :])
+    for j in range(residues):
+        part = lifted[:, j * count : (j + 1) * count, :].reshape(deep, outer_w.shape[1])
+        update_ref[j] = mul(left, part.astype(BF16)) * (1.0 / count)
+
+
+def pair_kernel(n, *refs):
+    pairs, packets, refs = refs[:n], refs[n : 2 * n], refs[2 * n :]
+    update, proj, gates, gate_out, w_out, out_ref, state, one, right_at, left_at, valid = refs
+    res_dev, residues, width = pairs[0].shape
+    me = lax.axis_index("axial")
+    for r in range(n):
+        owner = lax.rem(me + r, n)
+        size = res_dev * residues
+        state[pl.ds(pl.multiple_of(owner * size, size), size), :] = (
+            pairs[r][...].astype(F32).reshape(size, width)
+        )
+        valid[pl.ds(pl.multiple_of(owner * res_dev, res_dev), res_dev), :] = packets[r][
+            ...
+        ].astype(F32)[residues : residues + res_dev, :residues]
+    for k in range(residues):
+        one[k * residues : (k + 1) * residues, :] = (
+            state[pl.ds(k, residues, stride=residues), :] + update[k]
+        )
+
+    choose = zero_one(
+        iota((residues, residues * C_TRI), 1) // C_TRI == iota((residues, residues * C_TRI), 0)
+    )
+    shown = mul(valid[...].astype(BF16), choose)
+    right_w = jnp.concatenate([proj[:, C_TRI:], gates[:, C_TRI:]], axis=1)
+    step = 8
+    for k in range(0, residues, step):
+        here = slice(k * residues, (k + step) * residues)
+        both = mul(normal(one[here, :]).astype(BF16), right_w)
+        both = sigmoid(both[:, C_TRI:]) * both[:, :C_TRI]
+        for p in range(step):
+            part = both[p * residues : (p + 1) * residues]
+            part = part * shown[:, (k + p) * C_TRI : (k + p + 1) * C_TRI]
+            right_at[(k + p) * residues : (k + p + 1) * residues, :] = part.astype(BF16).astype(F32)
+
+    own = jnp.concatenate(
+        [one[pl.ds(me * res_dev + i, residues, stride=residues), :] for i in range(res_dev)],
+        axis=0,
+    )
+    left_w = jnp.concatenate([proj[:, :C_TRI], gates[:, :C_TRI], gate_out[...]], axis=1)
+    own_all = mul(normal(own).astype(BF16), left_w)
+    own_gate = sigmoid(own_all[:, 2 * C_TRI :])
+    left = sigmoid(own_all[:, C_TRI : 2 * C_TRI]) * own_all[:, :C_TRI]
+    own_valid = packets[0][...].astype(F32)[residues : residues + res_dev, :residues].astype(BF16)
+    choose = zero_one(
+        iota((res_dev, res_dev * C_TRI), 1) // C_TRI == iota((res_dev, res_dev * C_TRI), 0)
+    )
+    shown = mul(own_valid, choose, ((0,), (0,)))
+    for i in range(res_dev):
+        part = left[i * residues : (i + 1) * residues] * shown[:, i * C_TRI : (i + 1) * C_TRI]
+        left_at[i * residues : (i + 1) * residues, :] = part.astype(BF16).astype(F32)
+    sums = [jnp.zeros((residues, C_TRI), F32) for _ in range(res_dev)]
+    for k in range(residues):
+        other = right_at[k * residues : (k + 1) * residues, :]
+        for i in range(res_dev):
+            sums[i] += left_at[i * residues + k : i * residues + k + 1, :] * other
+    mixed = normal(jnp.concatenate(sums, axis=0)).astype(BF16)
+    result = own + own_gate * mul(mixed, w_out[...])
+    out_ref[...] = result.reshape(res_dev, residues, width).astype(BF16)
+
+
+def call(kernel, out_shape, scratch, cost, *args):
+    flops, moved = cost
+    return pl.pallas_call(
+        kernel,
+        out_shape=out_shape,
+        in_specs=[pl.BlockSpec(memory_space=pltpu.VMEM)] * len(args),
+        out_specs=jax.tree.map(lambda _: pl.BlockSpec(memory_space=pltpu.VMEM), out_shape),
+        scratch_shapes=scratch,
+        compiler_params=pltpu.CompilerParams(vmem_limit_bytes=VMEM_LIMIT),
+        cost_estimate=pl.CostEstimate(flops=flops, bytes_accessed=moved, transcendentals=0),
+    )(*args)
+
+
+def from_all(array, n):
+    return [array] + [
+        lax.ppermute(array, "axial", [(i, (i - r) % n) for i in range(n)]) for r in range(1, n)
+    ]
+
+
+def local_whole(
+    homolog_activity,
+    homolog_symbol_ids,
+    residue_present_mask,
+    pair_state,
+    pair_valid_mask,
+    symbol_lookup_matrix,
+    row_query_weight,
+    horizontal_attention_matrix,
+    pair_bias_weight,
+    horizontal_final_matrix,
+    column_query_weight,
+    vertical_attention_matrix,
+    vertical_final_matrix,
+    tensor_mean_lift_matrix,
+    outer_product_output_weight,
+    triangle_projection_weight,
+    triangle_projection_gate,
+    triangle_output_gate,
+    triangle_output_weight,
+):
+    n = lax.axis_size("axial")
+    per, residues, width = homolog_activity.shape
+    res_dev, _, pair_width = pair_state.shape
+    count = per * n
+    rows = packet_rows(residues, res_dev)
+    acts = from_all(homolog_activity, n)
+    packet = call(
+        packet_kernel,
+        jax.ShapeDtypeStruct((rows, 128), BF16),
+        [pltpu.VMEM((rows, 128), F32)],
+        (2 * 10**7, 10**5),
+        pair_state,
+        homolog_symbol_ids,
+        pair_valid_mask,
+        pair_bias_weight,
+    )
+    packets = from_all(packet, n)
+    pairs = from_all(pair_state, n)
+    alignment, update = call(
+        functools.partial(msa_kernel, n),
+        (
+            jax.ShapeDtypeStruct((count, res_dev, width), BF16),
+            jax.ShapeDtypeStruct((residues, residues, pair_width), F32),
+        ),
+        [
+            pltpu.VMEM((count * residues, width), F32),
+            pltpu.VMEM((MEAN_HIDDEN_SIZE, count * residues, pair_width), F32),
+        ],
+        (10**9, 2 * 10**6),
+        *acts,
+        *packets,
+        residue_present_mask.reshape(1, residues),
+        symbol_lookup_matrix,
+        row_query_weight,
+        horizontal_attention_matrix,
+        horizontal_final_matrix,
+        column_query_weight,
+        vertical_attention_matrix,
+        vertical_final_matrix,
+        tensor_mean_lift_matrix,
+        outer_product_output_weight,
+    )
+    pair_output = call(
+        functools.partial(pair_kernel, n),
+        jax.ShapeDtypeStruct((res_dev, residues, pair_width), BF16),
+        [
+            pltpu.VMEM((residues * residues, pair_width), F32),
+            pltpu.VMEM((residues * residues, pair_width), F32),
+            pltpu.VMEM((residues * residues, C_TRI), F32),
+            pltpu.VMEM((res_dev * residues, C_TRI), F32),
+            pltpu.VMEM((residues, residues), F32),
+        ],
+        (3 * 10**8, 10**6),
+        *pairs,
+        *packets,
+        update,
+        triangle_projection_weight,
+        triangle_projection_gate,
+        triangle_output_gate,
+        triangle_output_weight,
+    )
+    return (alignment, pair_output)
+
+
+def local(homolog_activity, homolog_symbol_ids, residue_present_mask, pair_state, *others):
+    n = lax.axis_size("axial")
+    per, residues, _ = homolog_activity.shape
+    small = per * n == 8 and residues == 32 and pair_state.shape[0] == 8
+    plan = local_whole if small else local_sharded
+    return plan(homolog_activity, homolog_symbol_ids, residue_present_mask, pair_state, *others)
+
+
 def solution(mesh):
+    parts, copied = P(("dp", "axial")), P()
     return jax.shard_map(
         local,
         mesh=mesh,
-        in_specs=(
-            P(("dp", "axial"), None, None),
-            P(("dp", "axial"), None),
-            P("dp"),
-            P(("dp", "axial"), None, None),
-            P(("dp", "axial"), None),
-            P(),
-            P(),
-            P(),
-            P(),
-            P(),
-            P(),
-            P(),
-            P(),
-            P(),
-            P(),
-            P(),
-            P(),
-            P(),
-            P(),
-        ),
+        in_specs=(parts, parts, P("dp"), parts, parts) + (copied,) * 14,
         out_specs=(P("dp", "axial", None), P(("dp", "axial"), None, None)),
         check_vma=False,
     )

time: 104 us -> 35.9 us (0.35)
  blocking collectives: 36.1 us -> 0 us
  matrix products: 17 us -> 0 us
  waiting for transfers between devices: 15.8 us -> 1.62 us
  Pallas kernels: 0 us -> 7.11 us
  other arithmetic: 6.46 us -> 0 us
  local copies, waits for them, and re-layouts: 14.8 us -> 8.95 us
  starting transfers between devices: 11.3 us -> 17 us
    all_gather x2 -> x0, blocking collectives: 28 us -> none  [the longest x1 14.9 us: local(): bias_full = lax.all_gather(bias_rows, 'axial', axis=1, tiled=True)]
    ppermute x0 -> x9, starting transfers between devices: none -> 17 us  [from_all(): lax.ppermute(array, 'axial', [(i, (i - r) % n) for i in range(n)])]
    all_to_all x3 -> x0, waiting for transfers between devices: 15.8 us -> none  [the longest x1 5.65 us: local(): lax.all_to_all(homolog_across_update, 'axial', split_axis=1, concat_axis=...]
    dot_general x47 -> x0, matrix products: 15.7 us -> none  [the longest x9 2.86 us: gated_attend(): jnp.einsum('bhij,bjhd->bihd', weights, attended_entries, preferred_elemen...]
    all_to_all x3 -> x0, starting transfers between devices: 11.3 us -> none  [the longest x1 4.74 us: local(): lax.all_to_all(homolog_across_update, 'axial', split_axis=1, concat_axis=...]
    all_to_all x1 -> x0, blocking collectives: 8.11 us -> none  [local(): lax.all_to_all(partial_sum.astype(jnp.bfloat16), 'axial', split_axis=1, c...]
    pallas_call x0 -> x3, Pallas kernels: none -> 7.11 us  [call(): pl.pallas_call(kernel, out_shape=out_shape, in_specs=[pl.BlockSpec(memory...]
    unnamed x34 -> x38, local copies, waits for them, and re-layouts: 2.77 us -> 8.95 us
  transfers between devices with their start and end apart: 3 -> 9, of which waited for: 3 -> 3; matrix products, arithmetic and copies ran while one was open for 1% -> 5% of each run, Pallas kernels for 0% -> 14%
where the time goes in v1:
time: 35.9 us; the launch traced here: 35.5 us
  starting transfers between devices  17 us (47%)
  local copies, waits for them, and re-layouts  8.95 us (25%)
  Pallas kernels  7.11 us (20%)
  waiting for transfers between devices  1.62 us (5%)
  between operations  0.8 us (2%)
    ppermute x9, starting transfers between devices, from_all(): lax.ppermute(array, 'axial', [(i, (i - r) % n) for i in range(n)])  17 us
    unnamed x38, local copies, waits for them, and re-layouts  8.95 us
    pallas_call x3, Pallas kernels, call(): pl.pallas_call(kernel, out_shape=out_shape, in_specs=[pl.BlockSpec(memory...  7.11 us
    ppermute x9, waiting for transfers between devices, from_all(): lax.ppermute(array, 'axial', [(i, (i - r) % n) for i in range(n)])  1.62 us
  transfers between devices with their start and end apart: 9, of which 3 were waited for; matrix products, arithmetic and copies ran while one was open for 5% of the time, Pallas kernels for 14%

profile of v1, /device:TPU:0, one launch (start us, length us, event | category | flops | bytes accessed | tf_op | source)
XLA Modules:
  0.0 35.5 jit_solution(15016066018720653358)
XLA Ops:
  0.7 5.1 %collective-permute-start = (bf16[2,32,256]{2,1,0:T(8,128)(2,1)}, bf16[2,32,256]{2,1,0:T(8,128)(2,1)S(1)}, u32[]{:S(2)}, u32[]{:S(2)}) collective-permute-start(bf16[2,32,256]{2,1,0:T(8,128)(2,1)} %refs_0_.2), channel_id=1, source_target_pairs={{0,3},{1,0},{2,1},{3,2},{4,7},{5,4},{6,5},{7,6},{8,11},{9,8},{10,9... | collective-permute-start | bytes 98312 | tf_op jit(solution)/shard_map/ppermute | solution.py:466
  5.8 1.0 %collective-permute-start.2 = (bf16[2,32,256]{2,1,0:T(8,128)(2,1)}, bf16[2,32,256]{2,1,0:T(8,128)(2,1)S(1)}, u32[]{:S(2)}, u32[]{:S(2)}) collective-permute-start(bf16[2,32,256]{2,1,0:T(8,128)(2,1)} %refs_0_.2), channel_id=1, source_target_pairs={{0,1},{1,2},{2,3},{3,0},{4,5},{5,6},{6,7},{7,4},{8,9},{9,10},{10,1... | collective-permute-start | bytes 98312 | tf_op jit(solution)/shard_map/ppermute | solution.py:466
  6.8 0.8 %copy.21.weight_ref = bf16[128,8]{1,0:T(8,128)(2,1)S(1)} copy(bf16[128,8]{0,1:T(8,128)(2,1)} %param.27) | data formatting | bytes 4096 | tf_op args[8]
  7.6 0.8 %copy-done = bf16[8,32,128]{2,1,0:T(8,128)(2,1)S(1)} copy-done((bf16[8,32,128]{2,1,0:T(8,128)(2,1)S(1)}, bf16[8,32,128]{2,1,0:T(8,128)(2,1)}, u32[]{:S(2)}) %copy-start) | copy-done | bytes 65560
  8.4 0.4 %shard_map.194.refs_4_ = bf16[48,128]{1,0:T(8,128)(2,1)S(1)} custom-call(bf16[8,32,128]{2,1,0:T(8,128)(2,1)S(1)} %copy-done, s32[2,32]{1,0:T(2,128)S(1)} %copy-done.3, s32[8,32]{1,0:T(8,128)S(1)} %copy-done.2, bf16[128,8]{1,0:T(8,128)(2,1)S(1)} %copy.21.weight_ref), custom_call_target="tpu_custom_call" | custom-call | flops 20000000 | bytes 100000 | tf_op jit(solution)/shard_map/pallas_call | solution.py:453
  8.8 2.9 %collective-permute-start.3 = (bf16[48,128]{1,0:T(8,128)(2,1)S(1)}, bf16[48,128]{1,0:T(8,128)(2,1)S(1)}, u32[]{:S(2)}, u32[]{:S(2)}) collective-permute-start(bf16[48,128]{1,0:T(8,128)(2,1)S(1)} %shard_map.194.refs_4_), channel_id=1, source_target_pairs={{0,3},{1,0},{2,1},{3,2},{4,7},{5,4},{6,5},{7,6},{8,11},{9,8},{10,9... | collective-permute-start | bytes 36872 | tf_op jit(solution)/shard_map/ppermute | solution.py:466
  11.7 1.1 %collective-permute-start.4 = (bf16[48,128]{1,0:T(8,128)(2,1)S(1)}, bf16[48,128]{1,0:T(8,128)(2,1)S(1)}, u32[]{:S(2)}, u32[]{:S(2)}) collective-permute-start(bf16[48,128]{1,0:T(8,128)(2,1)S(1)} %shard_map.194.refs_4_), channel_id=1, source_target_pairs={{0,2},{1,3},{2,0},{3,1},{4,6},{5,7},{6,4},{7,5},{8,10},{9,11},{10,... | collective-permute-start | bytes 36872 | tf_op jit(solution)/shard_map/ppermute | solution.py:466
  12.8 0.3 collective-permute-done.3.refs_5_
  13.1 2.0 %collective-permute-start.5 = (bf16[48,128]{1,0:T(8,128)(2,1)S(1)}, bf16[48,128]{1,0:T(8,128)(2,1)S(1)}, u32[]{:S(2)}, u32[]{:S(2)}) collective-permute-start(bf16[48,128]{1,0:T(8,128)(2,1)S(1)} %shard_map.194.refs_4_), channel_id=1, source_target_pairs={{0,1},{1,2},{2,3},{3,0},{4,5},{5,6},{6,7},{7,4},{8,9},{9,10},{10,1... | collective-permute-start | bytes 36872 | tf_op jit(solution)/shard_map/ppermute | solution.py:466
  15.0 0.9 %copy.22.refs_16_ = bf16[256,64]{1,0:T(8,128)(2,1)S(1)} copy(bf16[256,64]{0,1:T(8,128)(2,1)} %param.32) | data formatting | bytes 65536 | tf_op args[13]
  15.9 0.5 %collective-permute-done.4.refs_6_ = bf16[48,128]{1,0:T(8,128)(2,1)S(1)} collective-permute-done((bf16[48,128]{1,0:T(8,128)(2,1)S(1)}, bf16[48,128]{1,0:T(8,128)(2,1)S(1)}, u32[]{:S(2)}, u32[]{:S(2)}) %collective-permute-start.4) | collective-permute-done | bytes 12320 | tf_op jit(solution)/shard_map/ppermute | solution.py:466
  16.4 1.7 %collective-permute-start.6 = (bf16[8,32,128]{2,1,0:T(8,128)(2,1)S(1)}, bf16[8,32,128]{2,1,0:T(8,128)(2,1)S(1)}, u32[]{:S(2)}, u32[]{:S(2)}) collective-permute-start(bf16[8,32,128]{2,1,0:T(8,128)(2,1)S(1)} %copy-done.1), channel_id=1, source_target_pairs={{0,3},{1,0},{2,1},{3,2},{4,7},{5,4},{6,5},{7,6},{8,11},{9,8},{10,9... | collective-permute-start | bytes 196616 | tf_op jit(solution)/shard_map/ppermute | solution.py:466
  18.1 0.8 %collective-permute-done.5.refs_7_ = bf16[48,128]{1,0:T(8,128)(2,1)S(1)} collective-permute-done((bf16[48,128]{1,0:T(8,128)(2,1)S(1)}, bf16[48,128]{1,0:T(8,128)(2,1)S(1)}, u32[]{:S(2)}, u32[]{:S(2)}) %collective-permute-start.5) | collective-permute-done | bytes 12320 | tf_op jit(solution)/shard_map/ppermute | solution.py:466
  19.0 0.2 collective-permute-start.7
  19.2 3.0 %collective-permute-start.8 = (bf16[8,32,128]{2,1,0:T(8,128)(2,1)S(1)}, bf16[8,32,128]{2,1,0:T(8,128)(2,1)S(1)}, u32[]{:S(2)}, u32[]{:S(2)}) collective-permute-start(bf16[8,32,128]{2,1,0:T(8,128)(2,1)S(1)} %copy-done.1), channel_id=1, source_target_pairs={{0,1},{1,2},{2,3},{3,0},{4,5},{5,6},{6,7},{7,4},{8,9},{9,10},{10,1... | collective-permute-start | bytes 196616 | tf_op jit(solution)/shard_map/ppermute | solution.py:466
  22.2 1.0 %copy-done.4 = bf16[256,768]{1,0:T(8,128)(2,1)S(1)} copy-done((bf16[256,768]{1,0:T(8,128)(2,1)S(1)}, bf16[256,768]{1,0:T(8,128)(2,1)}, u32[]{:S(2)}) %copy-start.4) | copy-done | bytes 393240
  23.2 1.0 %copy-done.5 = bf16[256,768]{1,0:T(8,128)(2,1)S(1)} copy-done((bf16[256,768]{1,0:T(8,128)(2,1)S(1)}, bf16[256,768]{1,0:T(8,128)(2,1)}, u32[]{:S(2)}) %copy-start.5) | copy-done | bytes 393240
  24.2 0.9 %copy-done.6 = bf16[1024,128]{1,0:T(8,128)(2,1)S(1)} copy-done((bf16[1024,128]{1,0:T(8,128)(2,1)S(1)}, bf16[1024,128]{1,0:T(8,128)(2,1)}, u32[]{:S(2)}) %copy-start.6) | copy-done | bytes 262168
  25.2 0.9 %copy-done.8 = bf16[256,256]{1,0:T(8,128)(2,1)S(1)} copy-done((bf16[256,256]{1,0:T(8,128)(2,1)S(1)}, bf16[256,256]{1,0:T(8,128)(2,1)}, u32[]{:S(2)}) %copy-start.8) | copy-done | bytes 131096
  26.1 0.9 %copy-done.9 = bf16[256,256]{1,0:T(8,128)(2,1)S(1)} copy-done((bf16[256,256]{1,0:T(8,128)(2,1)S(1)}, bf16[256,256]{1,0:T(8,128)(2,1)}, u32[]{:S(2)}) %copy-start.9) | copy-done | bytes 131096
  27.0 0.9 %copy-done.10 = bf16[256,256]{1,0:T(8,128)(2,1)S(1)} copy-done((bf16[256,256]{1,0:T(8,128)(2,1)S(1)}, bf16[256,256]{1,0:T(8,128)(2,1)}, u32[]{:S(2)}) %copy-start.10) | copy-done | bytes 131096
  27.9 0.8 %copy-done.13 = bf16[2,32,256]{2,1,0:T(8,128)(2,1)S(1)} copy-done((bf16[2,32,256]{2,1,0:T(8,128)(2,1)S(1)}, bf16[2,32,256]{2,1,0:T(8,128)(2,1)}, u32[]{:S(2)}) %copy-start.13) | copy-done | bytes 32792
  28.6 4.6 %shard_map.195 = (bf16[8,8,256]{2,1,0:T(8,128)(2,1)}, f32[32,32,128]{2,1,0:T(8,128)S(1)}) custom-call(bf16[2,32,256]{2,1,0:T(8,128)(2,1)S(1)} %copy-done.13, bf16[2,32,256]{2,1,0:T(8,128)(2,1)S(1)} %collective-permute-done.refs_1_, bf16[2,32,256]{2,1,0:T(8,128)(2,1)S(1)} %collective-permute-done.1.refs_2_, ...), custom_call_target="tpu_custom_call" | custom-call | flops 1000000000 | bytes 2000000 | tf_op jit(solution)/shard_map/pallas_call | solution.py:453
  33.3 2.2 %shard_map.196 = bf16[8,32,128]{2,1,0:T(8,128)(2,1)} custom-call(bf16[8,32,128]{2,1,0:T(8,128)(2,1)S(1)} %copy-done.1, bf16[8,32,128]{2,1,0:T(8,128)(2,1)S(1)} %collective-permute-done.6.refs_1_, bf16[8,32,128]{2,1,0:T(8,128)(2,1)S(1)} %collective-permute-done.7.refs_2_, bf16[8,32,128]{2,1,0:T(8,128)(2,1)S(1)} %collective-permute-done.8.refs_3_, ...), custom_call_target="tpu_custom_call" | custom-call | flops 300000000 | bytes 1000000 | tf_op jit(solution)/shard_map/pallas_call | solution.py:453
  (35 shorter events, 0.1 us)
Async XLA Ops:
  0.6 6.9 %copy-start.3 = (s32[2,32]{1,0:T(2,128)S(1)}, s32[2,32]{1,0:T(2,128)}, u32[]{:S(2)}) copy-start(s32[2,32]{1,0:T(2,128)} %ids_ref.1) | copy-start | bytes 772
  0.6 6.9 %copy-start.2 = (s32[8,32]{1,0:T(8,128)S(1)}, s32[8,32]{1,0:T(8,128)}, u32[]{:S(2)}) copy-start(s32[8,32]{1,0:T(8,128)} %valid_ref.1) | copy-start | bytes 3076
  0.7 18.5 %collective-permute-start = (bf16[2,32,256]{2,1,0:T(8,128)(2,1)}, bf16[2,32,256]{2,1,0:T(8,128)(2,1)S(1)}, u32[]{:S(2)}, u32[]{:S(2)}) collective-permute-start(bf16[2,32,256]{2,1,0:T(8,128)(2,1)} %refs_0_.2), channel_id=1, source_target_pairs={{0,3},{1,0},{2,1},{3,2},{4,7},{5,4},{6,5},{7,6},{8,11},{9,8},{10,9... | collective-permute-start | bytes 98312 | tf_op jit(solution)/shard_map/ppermute | solution.py:466
  5.8 16.4 %collective-permute-start.1 = (bf16[2,32,256]{2,1,0:T(8,128)(2,1)}, bf16[2,32,256]{2,1,0:T(8,128)(2,1)S(1)}, u32[]{:S(2)}, u32[]{:S(2)}) collective-permute-start(bf16[2,32,256]{2,1,0:T(8,128)(2,1)} %refs_0_.2), channel_id=1, source_target_pairs={{0,2},{1,3},{2,0},{3,1},{4,6},{5,7},{6,4},{7,5},{8,10},{9,11},{10,... | collective-permute-start | bytes 98312 | tf_op jit(solution)/shard_map/ppermute | solution.py:466
  5.8 16.4 %collective-permute-start.2 = (bf16[2,32,256]{2,1,0:T(8,128)(2,1)}, bf16[2,32,256]{2,1,0:T(8,128)(2,1)S(1)}, u32[]{:S(2)}, u32[]{:S(2)}) collective-permute-start(bf16[2,32,256]{2,1,0:T(8,128)(2,1)} %refs_0_.2), channel_id=1, source_target_pairs={{0,1},{1,2},{2,3},{3,0},{4,5},{5,6},{6,7},{7,4},{8,9},{9,10},{10,1... | collective-permute-start | bytes 98312 | tf_op jit(solution)/shard_map/ppermute | solution.py:466
  8.4 13.8 %copy-start.7 = (bf16[256,256]{1,0:T(8,128)(2,1)S(1)}, bf16[256,256]{1,0:T(8,128)(2,1)}, u32[]{:S(2)}) copy-start(bf16[256,256]{1,0:T(8,128)(2,1)} %refs_10_.2) | copy-start | bytes 393220
  8.8 7.6 %copy-start.1 = (bf16[8,32,128]{2,1,0:T(8,128)(2,1)S(1)}, bf16[8,32,128]{2,1,0:T(8,128)(2,1)}, u32[]{:S(2)}) copy-start(bf16[8,32,128]{2,1,0:T(8,128)(2,1)} %refs_0_.3) | copy-start | bytes 196612
  8.8 13.4 %copy-start.16 = (bf16[23,256]{1,0:T(8,128)(2,1)S(1)}, bf16[23,256]{1,0:T(8,128)(2,1)}, u32[]{:S(2)}) copy-start(bf16[23,256]{1,0:T(8,128)(2,1)} %refs_9_.2) | copy-start | bytes 35332
  8.8 4.3 %collective-permute-start.3 = (bf16[48,128]{1,0:T(8,128)(2,1)S(1)}, bf16[48,128]{1,0:T(8,128)(2,1)S(1)}, u32[]{:S(2)}, u32[]{:S(2)}) collective-permute-start(bf16[48,128]{1,0:T(8,128)(2,1)S(1)} %shard_map.194.refs_4_), channel_id=1, source_target_pairs={{0,3},{1,0},{2,1},{3,2},{4,7},{5,4},{6,5},{7,6},{8,11},{9,8},{10,9... | collective-permute-start | bytes 36872 | tf_op jit(solution)/shard_map/ppermute | solution.py:466
  11.7 4.7 %collective-permute-start.4 = (bf16[48,128]{1,0:T(8,128)(2,1)S(1)}, bf16[48,128]{1,0:T(8,128)(2,1)S(1)}, u32[]{:S(2)}, u32[]{:S(2)}) collective-permute-start(bf16[48,128]{1,0:T(8,128)(2,1)S(1)} %shard_map.194.refs_4_), channel_id=1, source_target_pairs={{0,2},{1,3},{2,0},{3,1},{4,6},{5,7},{6,4},{7,5},{8,10},{9,11},{10,... | collective-permute-start | bytes 36872 | tf_op jit(solution)/shard_map/ppermute | solution.py:466
  13.1 5.9 %collective-permute-start.5 = (bf16[48,128]{1,0:T(8,128)(2,1)S(1)}, bf16[48,128]{1,0:T(8,128)(2,1)S(1)}, u32[]{:S(2)}, u32[]{:S(2)}) collective-permute-start(bf16[48,128]{1,0:T(8,128)(2,1)S(1)} %shard_map.194.refs_4_), channel_id=1, source_target_pairs={{0,1},{1,2},{2,3},{3,0},{4,5},{5,6},{6,7},{7,4},{8,9},{9,10},{10,1... | collective-permute-start | bytes 36872 | tf_op jit(solution)/shard_map/ppermute | solution.py:466
  15.9 6.3 %copy-start.17 = (s32[32]{0:T(128)S(1)}, s32[32]{0:T(128)}, u32[]{:S(2)}) copy-start(s32[32]{0:T(128)} %param.21) | copy-start | bytes 388
  16.4 16.8 %collective-permute-start.6 = (bf16[8,32,128]{2,1,0:T(8,128)(2,1)S(1)}, bf16[8,32,128]{2,1,0:T(8,128)(2,1)S(1)}, u32[]{:S(2)}, u32[]{:S(2)}) collective-permute-start(bf16[8,32,128]{2,1,0:T(8,128)(2,1)S(1)} %copy-done.1), channel_id=1, source_target_pairs={{0,3},{1,0},{2,1},{3,2},{4,7},{5,4},{6,5},{7,6},{8,11},{9,8},{10,9... | collective-permute-start | bytes 196616 | tf_op jit(solution)/shard_map/ppermute | solution.py:466
  19.0 14.3 %collective-permute-start.7 = (bf16[8,32,128]{2,1,0:T(8,128)(2,1)S(1)}, bf16[8,32,128]{2,1,0:T(8,128)(2,1)S(1)}, u32[]{:S(2)}, u32[]{:S(2)}) collective-permute-start(bf16[8,32,128]{2,1,0:T(8,128)(2,1)S(1)} %copy-done.1), channel_id=1, source_target_pairs={{0,2},{1,3},{2,0},{3,1},{4,6},{5,7},{6,4},{7,5},{8,10},{9,11},{10,... | collective-permute-start | bytes 196616 | tf_op jit(solution)/shard_map/ppermute | solution.py:466
  19.2 14.1 %collective-permute-start.8 = (bf16[8,32,128]{2,1,0:T(8,128)(2,1)S(1)}, bf16[8,32,128]{2,1,0:T(8,128)(2,1)S(1)}, u32[]{:S(2)}, u32[]{:S(2)}) collective-permute-start(bf16[8,32,128]{2,1,0:T(8,128)(2,1)S(1)} %copy-done.1), channel_id=1, source_target_pairs={{0,1},{1,2},{2,3},{3,0},{4,5},{5,6},{6,7},{7,4},{8,9},{9,10},{10,1... | collective-permute-start | bytes 196616 | tf_op jit(solution)/shard_map/ppermute | solution.py:466
  22.2 1.0 %copy-start.4 = (bf16[256,768]{1,0:T(8,128)(2,1)S(1)}, bf16[256,768]{1,0:T(8,128)(2,1)}, u32[]{:S(2)}) copy-start(bf16[256,768]{1,0:T(8,128)(2,1)} %refs_11_.2) | copy-start | bytes 1179652
  23.2 1.0 %copy-start.5 = (bf16[256,768]{1,0:T(8,128)(2,1)S(1)}, bf16[256,768]{1,0:T(8,128)(2,1)}, u32[]{:S(2)}) copy-start(bf16[256,768]{1,0:T(8,128)(2,1)} %refs_14_.1) | copy-start | bytes 1179652
  24.2 0.9 %copy-start.6 = (bf16[1024,128]{1,0:T(8,128)(2,1)S(1)}, bf16[1024,128]{1,0:T(8,128)(2,1)}, u32[]{:S(2)}) copy-start(bf16[1024,128]{1,0:T(8,128)(2,1)} %refs_17_.1) | copy-start | bytes 786436
  25.2 0.9 %copy-start.8 = (bf16[256,256]{1,0:T(8,128)(2,1)S(1)}, bf16[256,256]{1,0:T(8,128)(2,1)}, u32[]{:S(2)}) copy-start(bf16[256,256]{1,0:T(8,128)(2,1)} %refs_12_.2) | copy-start | bytes 393220
  26.1 0.9 %copy-start.9 = (bf16[256,256]{1,0:T(8,128)(2,1)S(1)}, bf16[256,256]{1,0:T(8,128)(2,1)}, u32[]{:S(2)}) copy-start(bf16[256,256]{1,0:T(8,128)(2,1)} %refs_13_.1) | copy-start | bytes 393220
  28.6 4.6 %copy-start.11 = (bf16[128,256]{1,0:T(8,128)(2,1)S(1)}, bf16[128,256]{1,0:T(8,128)(2,1)}, u32[]{:S(2)}) copy-start(bf16[128,256]{1,0:T(8,128)(2,1)} %refs_9_.3) | copy-start | bytes 196612
  28.6 4.6 %copy-start.12 = (bf16[128,256]{1,0:T(8,128)(2,1)S(1)}, bf16[128,256]{1,0:T(8,128)(2,1)}, u32[]{:S(2)}) copy-start(bf16[128,256]{1,0:T(8,128)(2,1)} %refs_10_.3) | copy-start | bytes 196612
  28.6 4.6 %copy-start.14 = (bf16[128,128]{1,0:T(8,128)(2,1)S(1)}, bf16[128,128]{1,0:T(8,128)(2,1)}, u32[]{:S(2)}) copy-start(bf16[128,128]{1,0:T(8,128)(2,1)} %refs_11_.3) | copy-start | bytes 98308
  28.6 4.7 %copy-start.15 = (bf16[128,128]{1,0:T(8,128)(2,1)S(1)}, bf16[128,128]{1,0:T(8,128)(2,1)}, u32[]{:S(2)}) copy-start(bf16[128,128]{1,0:T(8,128)(2,1)} %refs_12_.3) | copy-start | bytes 98308
  (3 other events, 2.5 us)
